TPU v7x, 256 devices: a whole 4x4x8 slice. The times are simulated.
256 devices in a mesh: replica: 32 (over z, y), tensor: 8 (over x, core).
Axes of the slice: x: 4, y: 4, z: 8, core: 2. Of those that a mesh axis runs over, the one named last changes fastest.
Arguments:
- hidden: bfloat16 [8192, 8192], P('replica'), may hold values from -6 to 6
- key_value_weight: bfloat16 [8192, 2, 1024], P(None, None, 'tensor'), may hold values from -0.0625 to 0.0625
- adapter_down_weight: bfloat16 [128, 8192, 128], P('replica', 'tensor'), may hold values from -0.0625 to 0.0625
- adapter_up_weight: bfloat16 [128, 2, 64, 1024], P('replica', None, None, 'tensor'), may hold values from -0.75 to 0.75
- token_adapter_index: int32 [8192], P('replica'), may hold values from 0 to 127, as said below
- destinations: int32 [8192, 1], P('replica'), may hold values from 0 to 31; in each aligned block of 256 rows (0 to 255, 256 to 511, ...) at most 16 rows name the same one
Outputs:
- kv_cache: bfloat16 [16384, 2, 1024], P('replica', None, 'tensor')
Inputs may be any that keep to these rules, and one draw needn't show every extreme that they name: `token_adapter_index`: adapter a is stored on replica a // 4. The tokens arriving on one replica use exactly 8 distinct adapters, no two of them stored on the same replica. `destinations`: among the tokens arriving on one replica at most 16 have the same destination.
All inputs are finite; a program needn't handle non-finite values.
Results may differ from a plain program's by a relative error of at most 0.0029.
Values may be sent and summed in bfloat16 or wider, within the bound.
A program may use at most 128 MiB of HBM per device.

v0:
```python
import jax
import jax.numpy as jnp
from jax import lax
from jax.sharding import PartitionSpec as P

USE = 8


adapter_scale = 0.5


def blockwise_shrink(source_hidden, slot_down, source_row, block_slot, block_count, block_rows):

    def one_block(carried_state, loop_element):
        row_ids, slot_number = loop_element
        rows = jnp.take(source_hidden, row_ids, axis=0)
        weight = lax.dynamic_index_in_dim(slot_down, slot_number, 0, keepdims=False)
        return (carried_state, jnp.dot(rows, weight, preferred_element_type=jnp.float32))

    closing_state, results = lax.scan(
        one_block, jnp.float32(0.0), (source_row.reshape(block_count, block_rows), block_slot)
    )
    return results


def shards(
    hidden,
    key_value_weight,
    adapter_down_weight,
    adapter_up_weight,
    token_adapter_index,
    destinations,
):
    block_rows = 128
    replicas = lax.axis_size("replica")
    use_count = USE
    row_count = hidden.shape[0]
    model_width = hidden.shape[1]
    head_cols = key_value_weight.shape[2]
    holder_count = adapter_down_weight.shape[0]
    adapter_rank_width = adapter_up_weight.shape[2]
    owner_of = token_adapter_index // holder_count
    local_index = token_adapter_index % holder_count
    peer_ids = jnp.arange(replicas, dtype=jnp.int32)
    owner_match = owner_of[:, None] == peer_ids[None, :]
    present = jnp.any(owner_match, axis=0)
    requests = jnp.max(jnp.where(owner_match, local_index[:, None], -1), axis=0)
    order_rank = jnp.cumsum(present.astype(jnp.int32)) - 1
    slot_of_owner = jnp.where(present, order_rank, 0)
    row_slot = jnp.sum(jnp.where(owner_match, slot_of_owner[None, :], 0), axis=1)
    slot_ids = jnp.arange(use_count, dtype=jnp.int32)
    owner_list = jnp.sum(
        jnp.where(
            (order_rank[None, :] == slot_ids[:, None]) & present[None, :], peer_ids[None, :], 0
        ),
        axis=1,
    )
    asked_for = lax.all_to_all(
        requests.reshape(replicas, 1), "replica", split_axis=0, concat_axis=0, tiled=True
    )[:, 0]
    active_mask = asked_for >= 0
    selected_index = jnp.maximum(asked_for, 0)
    outbound_down = jnp.where(
        active_mask[:, None, None], jnp.take(adapter_down_weight, selected_index, axis=0), 0
    )
    outbound_up = jnp.where(
        active_mask[:, None, None, None], jnp.take(adapter_up_weight, selected_index, axis=0), 0
    )
    got_down, got_up = (
        lax.all_to_all(outbound_down, "replica", split_axis=0, concat_axis=0, tiled=True),
        lax.all_to_all(outbound_up, "replica", split_axis=0, concat_axis=0, tiled=True),
    )
    base_projection = jnp.dot(
        hidden,
        key_value_weight.reshape(model_width, 2 * head_cols),
        preferred_element_type=jnp.float32,
    )
    base_projection = base_projection.reshape(row_count, 2, head_cols)
    fetched_down = jnp.take(got_down, owner_list, axis=0)
    fetched_up = jnp.take(got_up, owner_list, axis=0)
    membership = (row_slot[:, None] == slot_ids[None, :]).astype(jnp.int32)
    slot_counts = jnp.sum(membership, axis=0)
    padded_counts = (slot_counts + block_rows - 1) // block_rows * block_rows
    slot_ends = jnp.cumsum(padded_counts)
    slot_starts = slot_ends - padded_counts
    within_slot = jnp.sum((jnp.cumsum(membership, axis=0) - 1) * membership, axis=1)
    position = jnp.sum(membership * slot_starts[None, :], axis=1) + within_slot
    block_count = row_count // block_rows + use_count
    source_row = jnp.full((block_count * block_rows,), row_count, jnp.int32)
    source_row = source_row.at[position].set(jnp.arange(row_count, dtype=jnp.int32))
    block_first = jnp.arange(block_count, dtype=jnp.int32) * block_rows
    block_slot = jnp.minimum(
        jnp.sum((block_first[:, None] >= slot_ends[None, :]).astype(jnp.int32), axis=1),
        use_count - 1,
    )
    padded_hidden = jnp.concatenate([hidden, jnp.zeros((1, model_width), jnp.bfloat16)], axis=0)
    whole_down = lax.all_gather(fetched_down, "tensor", axis=1, tiled=True)
    shrink = blockwise_shrink(
        padded_hidden, whole_down, source_row, block_slot, block_count, block_rows
    )
    shrink = shrink.astype(jnp.bfloat16)
    block_up = jnp.take(fetched_up, block_slot, axis=0)
    rank_pairs = shrink.reshape(block_count, block_rows, 2, adapter_rank_width)
    delta_block = jnp.einsum(
        "bnpr,bprc->bnpc", rank_pairs, block_up, preferred_element_type=jnp.float32
    )
    update_row_values = jnp.take(
        delta_block.reshape(block_count * block_rows, 2, head_cols), position, axis=0
    )
    projected_output = (base_projection + adapter_scale * update_row_values).astype(jnp.bfloat16)
    dest_rank = destinations[:, 0]
    dest_marks = (dest_rank[:, None] == peer_ids[None, :]).astype(jnp.int32)
    within_dest = jnp.sum((jnp.cumsum(dest_marks, axis=0) - 1) * dest_marks, axis=1)
    capacity = 2 * row_count // replicas
    outgoing = (
        jnp.zeros((replicas, capacity, 2, head_cols), jnp.bfloat16)
        .at[dest_rank, within_dest]
        .set(projected_output)
    )
    incoming = lax.all_to_all(outgoing, "replica", split_axis=0, concat_axis=0, tiled=True)
    return incoming.reshape(replicas * capacity, 2, head_cols)


def solution(mesh):
    placed = (
        P("replica", None),
        P(None, None, "tensor"),
        P("replica", "tensor", None),
        P("replica", None, None, "tensor"),
        P("replica"),
        P("replica", None),
    )
    return jax.shard_map(
        shards, mesh=mesh, in_specs=placed, out_specs=P("replica", None, "tensor"), check_vma=False
    )
```

profile of v0, /device:TPU:64, one launch (start us, length us, event | category | flops | bytes accessed | tf_op | source)
XLA Modules:
  0.0 496.2 jit_solution(10206074176939181229)
XLA Ops:
  7.9 18.4 %all_to_all.24 = s32[32,1,1]{2,1,0:T(1,128)S(1)} all-to-all(s32[32,1,1]{2,1,0:T(1,128)S(1)} %copy.39), channel_id=1, replica_groups=mesh['replica'=32,'tensor'=8] {'replica'}, dimensions={0} | all-to-all | bytes 256 | tf_op jit(solution)/shard_map/all_to_all | solution.py:58
  33.0 7.6 %select_select_fusion = bf16[32,1024,128]{2,1,0:T(8,128)(2,1)} fusion(bf16[32,1024,128]{2,1,0:T(8,128)(2,1)} %gather_fusion.4, pred[32]{0:T(512)(128)(4,1)S(1)} %get-tuple-element.39, pred[32]{0:T(512)(128)(4,1)S(1)} %get-tuple-element.38), kind=kLoop, calls=%fused_computation.25 | loop fusion | flops 8388608 | bytes 16777280 | tf_op jit(solution)/shard_map/jit(_where)/select_n | solution.py:63
  40.6 6.8 %all-to-all-start.2 = ((bf16[32,1024,128]{2,1,0:T(8,128)(2,1)}), bf16[32,1024,128]{2,1,0:T(8,128)(2,1)}, u32[]{:S(2)}, u32[]{:S(2)}) async-start(bf16[32,1024,128]{2,1,0:T(8,128)(2,1)} %select_select_fusion), calls=%async_computation.2 | async-start | bytes 16777216 | tf_op jit(solution)/shard_map/all_to_all | solution.py:70
  47.7 185.0 %all-to-all-done.2 = bf16[32,1024,128]{2,1,0:T(8,128)(2,1)} async-done(((bf16[32,1024,128]{2,1,0:T(8,128)(2,1)}), bf16[32,1024,128]{2,1,0:T(8,128)(2,1)}, u32[]{:S(2)}, u32[]{:S(2)}) %all-to-all-start.2) | async-done | bytes 8388640 | tf_op jit(solution)/shard_map/all_to_all | solution.py:70
  242.3 10.1 %all-to-all-start.1 = ((bf16[32,2,64,128]{3,2,1,0:T(8,128)(2,1)}), bf16[32,2,64,128]{3,2,1,0:T(8,128)(2,1)S(1)}, u32[]{:S(2)}, u32[]{:S(2)}) async-start(bf16[32,2,64,128]{3,2,1,0:T(8,128)(2,1)} %select_select_fusion.1), calls=%async_computation.1 | async-start | bytes 2097152 | tf_op jit(solution)/shard_map/all_to_all | solution.py:71
  252.6 5.6 %copy.56 = bf16[1024,8,2,128]{3,1,2,0:T(8,128)(2,1)} copy(bf16[1024,8,2,128]{3,2,1,0:T(2,128)(2,1)} %bitcast.108) | data formatting | bytes 8388608
  258.2 6.4 %copy.37 = bf16[256,8192]{1,0:T(8,128)(2,1)} copy(bf16[256,8192]{0,1:T(8,128)(2,1)} %bitcast.106) | data formatting | bytes 8388608 | tf_op jit(solution)/shard_map/dot_general | solution.py:73
  264.7 4.8 concatenate.7
  271.5 8.1 %all-to-all-done.1 = bf16[32,2,64,128]{3,2,1,0:T(8,128)(2,1)S(1)} async-done(((bf16[32,2,64,128]{3,2,1,0:T(8,128)(2,1)}), bf16[32,2,64,128]{3,2,1,0:T(8,128)(2,1)S(1)}, u32[]{:S(2)}, u32[]{:S(2)}) %all-to-all-start.1) | async-done | bytes 1048608 | tf_op jit(solution)/shard_map/all_to_all | solution.py:71
  280.9 46.8 %all-gather.2.cloned.1.call-done = bf16[8,8192,128]{2,1,0:T(8,128)(2,1)} async-done(((bf16[8,1024,128]{2,1,0:T(8,128)(2,1)}), bf16[8,8192,128]{2,1,0:T(8,128)(2,1)}) %all-gather.2.cloned.1.call-update) | async-done | bytes 16777232 | tf_op jit(solution)/shard_map/all_gather | solution.py:97
  327.6 117.9 %while.10 = (s32[]{:T(128)}, bf16[10,128,128]{1,2,0:T(8,128)(2,1)S(1)}, s32[10,128]{1,0:T(8,128)S(1)}, bf16[257,8192]{1,0:T(8,128)(2,1)}, s32[10]{0:T(128)S(1)},...) while((s32[]{:T(128)}, bf16[10,128,128]{1,2,0:T(8,128)(2,1)S(1)}, ...), condition=%wide.region_17.18_spmd, body=%wide.region_16.17_spmd.sunk | while | flops 269486208 | bytes 8462103 | solution.py:20
  330.2 6.5 %gather_fusion = bf16[128,8192]{1,0:T(8,128)(2,1)S(1)} fusion(bf16[257,8192]{1,0:T(8,128)(2,1)} %get-tuple-element.118, s32[1024]{0:T(1024)S(1)} %pad_clamp_fusion.6), kind=kCustom, calls=%fused_computation.clone.1 | custom fusion | bytes 4194816 | tf_op jit(solution)/shard_map/while/body/eval_jaxpr/jit(_take)/gather | solution.py:16
  342.0 6.5 %gather_fusion = bf16[128,8192]{1,0:T(8,128)(2,1)S(1)} fusion(bf16[257,8192]{1,0:T(8,128)(2,1)} %get-tuple-element.118, s32[1024]{0:T(1024)S(1)} %pad_clamp_fusion.6), kind=kCustom, calls=%fused_computation.clone.1 | custom fusion | bytes 4194816 | tf_op jit(solution)/shard_map/while/body/eval_jaxpr/jit(_take)/gather | solution.py:16
  353.8 6.5 %gather_fusion = bf16[128,8192]{1,0:T(8,128)(2,1)S(1)} fusion(bf16[257,8192]{1,0:T(8,128)(2,1)} %get-tuple-element.118, s32[1024]{0:T(1024)S(1)} %pad_clamp_fusion.6), kind=kCustom, calls=%fused_computation.clone.1 | custom fusion | bytes 4194816 | tf_op jit(solution)/shard_map/while/body/eval_jaxpr/jit(_take)/gather | solution.py:16
  365.6 6.5 %gather_fusion = bf16[128,8192]{1,0:T(8,128)(2,1)S(1)} fusion(bf16[257,8192]{1,0:T(8,128)(2,1)} %get-tuple-element.118, s32[1024]{0:T(1024)S(1)} %pad_clamp_fusion.6), kind=kCustom, calls=%fused_computation.clone.1 | custom fusion | bytes 4194816 | tf_op jit(solution)/shard_map/while/body/eval_jaxpr/jit(_take)/gather | solution.py:16
  377.4 6.5 %gather_fusion = bf16[128,8192]{1,0:T(8,128)(2,1)S(1)} fusion(bf16[257,8192]{1,0:T(8,128)(2,1)} %get-tuple-element.118, s32[1024]{0:T(1024)S(1)} %pad_clamp_fusion.6), kind=kCustom, calls=%fused_computation.clone.1 | custom fusion | bytes 4194816 | tf_op jit(solution)/shard_map/while/body/eval_jaxpr/jit(_take)/gather | solution.py:16
  389.2 6.5 %gather_fusion = bf16[128,8192]{1,0:T(8,128)(2,1)S(1)} fusion(bf16[257,8192]{1,0:T(8,128)(2,1)} %get-tuple-element.118, s32[1024]{0:T(1024)S(1)} %pad_clamp_fusion.6), kind=kCustom, calls=%fused_computation.clone.1 | custom fusion | bytes 4194816 | tf_op jit(solution)/shard_map/while/body/eval_jaxpr/jit(_take)/gather | solution.py:16
  400.9 6.5 %gather_fusion = bf16[128,8192]{1,0:T(8,128)(2,1)S(1)} fusion(bf16[257,8192]{1,0:T(8,128)(2,1)} %get-tuple-element.118, s32[1024]{0:T(1024)S(1)} %pad_clamp_fusion.6), kind=kCustom, calls=%fused_computation.clone.1 | custom fusion | bytes 4194816 | tf_op jit(solution)/shard_map/while/body/eval_jaxpr/jit(_take)/gather | solution.py:16
  412.7 6.5 %gather_fusion = bf16[128,8192]{1,0:T(8,128)(2,1)S(1)} fusion(bf16[257,8192]{1,0:T(8,128)(2,1)} %get-tuple-element.118, s32[1024]{0:T(1024)S(1)} %pad_clamp_fusion.6), kind=kCustom, calls=%fused_computation.clone.1 | custom fusion | bytes 4194816 | tf_op jit(solution)/shard_map/while/body/eval_jaxpr/jit(_take)/gather | solution.py:16
  424.5 6.5 %gather_fusion = bf16[128,8192]{1,0:T(8,128)(2,1)S(1)} fusion(bf16[257,8192]{1,0:T(8,128)(2,1)} %get-tuple-element.118, s32[1024]{0:T(1024)S(1)} %pad_clamp_fusion.6), kind=kCustom, calls=%fused_computation.clone.1 | custom fusion | bytes 4194816 | tf_op jit(solution)/shard_map/while/body/eval_jaxpr/jit(_take)/gather | solution.py:16
  436.3 6.5 %gather_fusion = bf16[128,8192]{1,0:T(8,128)(2,1)S(1)} fusion(bf16[257,8192]{1,0:T(8,128)(2,1)} %get-tuple-element.118, s32[1024]{0:T(1024)S(1)} %pad_clamp_fusion.6), kind=kCustom, calls=%fused_computation.clone.1 | custom fusion | bytes 4194816 | tf_op jit(solution)/shard_map/while/body/eval_jaxpr/jit(_take)/gather | solution.py:16
  451.8 4.8 fusion.24
  457.0 10.0 %scatter_fusion = bf16[32,16,2,128]{3,2,1,0:T(2,128)(2,1)S(1)} fusion(bf16[32,16,2,128]{3,2,1,0:T(2,128)(2,1)S(1)} %broadcast_in_dim.165, s32[256]{0:T(256)S(1)} %bitcast.105, bf16[256,2,128]{2,1,0:T(2,128)(2,1)S(1)} %copy.44), kind=kCustom, calls=%fused_computation.8 | custom fusion | bytes 395264 | tf_op jit(solution)/shard_map/scatter | solution.py:118
  466.9 21.7 %all_to_all.25 = bf16[32,16,2,128]{3,2,1,0:T(2,128)(2,1)S(1)} all-to-all(bf16[32,16,2,128]{3,2,1,0:T(2,128)(2,1)S(1)} %scatter_fusion), channel_id=1, replica_groups=mesh['replica'=32,'tensor'=8] {'replica'}, dimensions={0} | all-to-all | bytes 524288 | tf_op jit(solution)/shard_map/all_to_all | solution.py:120
  (123 shorter events, 61.1 us)
Async XLA Ops:
  6.5 20.5 %copy-start = (bf16[4,1024,128]{2,1,0:T(8,128)(2,1)S(1)}, bf16[4,1024,128]{2,1,0:T(8,128)(2,1)}, u32[]{:S(2)}) copy-start(bf16[4,1024,128]{2,1,0:T(8,128)(2,1)} %param.10) | copy-start | bytes 3145732
  40.6 192.0 %all-to-all-start.2 = ((bf16[32,1024,128]{2,1,0:T(8,128)(2,1)}), bf16[32,1024,128]{2,1,0:T(8,128)(2,1)}, u32[]{:S(2)}, u32[]{:S(2)}) async-start(bf16[32,1024,128]{2,1,0:T(8,128)(2,1)} %select_select_fusion), calls=%async_computation.2 | async-start | bytes 16777216 | tf_op jit(solution)/shard_map/all_to_all | solution.py:70
  47.5 280.2 %all-gather.2.cloned.1.call-start = ((), (), s32[]{:S(2)}) async-start(), calls=%async_computation.4 | async-start | bytes 18874368 | tf_op jit(solution)/shard_map/all_gather | solution.py:97
  237.0 2.6 copy-start.3
  237.0 3.4 copy-start.2
  242.3 37.3 %all-to-all-start.1 = ((bf16[32,2,64,128]{3,2,1,0:T(8,128)(2,1)}), bf16[32,2,64,128]{3,2,1,0:T(8,128)(2,1)S(1)}, u32[]{:S(2)}, u32[]{:S(2)}) async-start(bf16[32,2,64,128]{3,2,1,0:T(8,128)(2,1)} %select_select_fusion.1), calls=%async_computation.1 | async-start | bytes 2097152 | tf_op jit(solution)/shard_map/all_to_all | solution.py:71
  252.6 5.6 %copy-start.4 = (s32[8,3]{0,1:T(4,128)}, s32[8,3]{0,1:T(4,128)S(1)}, u32[]{:S(2)}) copy-start(s32[8,3]{0,1:T(4,128)S(1)} %reduce-window.39) | copy-start | bytes 292
  264.7 4.8 slice-start
  451.8 37.5 %copy-start.1 = (bf16[4,1024,128]{2,1,0:T(8,128)(2,1)S(1)}, bf16[4,1024,128]{2,1,0:T(8,128)(2,1)}, u32[]{:S(2)}) copy-start(bf16[4,1024,128]{2,1,0:T(8,128)(2,1)} %param.10) | copy-start | bytes 3145732
Sparse Core Ops, SparseCore 0:
  238.8 88.8 all-gather.1
where the time goes:
time: 500 us; the launch traced here: 496 us
  waiting for transfers between devices  240 us (48%)
  local copies, waits for them, and re-layouts  118 us (24%)
  blocking collectives  40.1 us (8%)
  matrix products  31.5 us (6%)
  loops' own time  19.9 us (4%)
  starting transfers between devices  16.9 us (3%)
  other arithmetic  16 us (3%)
  between operations  13.7 us (3%)
    all_to_all x1, waiting for transfers between devices, shards(): lax.all_to_all(outbound_down, 'replica', split_axis=0, concat_axis=0, til...  185 us
    gather x10, local copies, waits for them, and re-layouts, one_block(): rows = jnp.take(source_hidden, row_ids, axis=0)  65.4 us
    all_gather x1, waiting for transfers between devices, shards(): whole_down = lax.all_gather(fetched_down, 'tensor', axis=1, tiled=True)  46.8 us
    dot_general x10, matrix products, one_block(): jnp.dot(rows, weight, preferred_element_type=jnp.float32)  26.3 us
    all_to_all x1, blocking collectives, shards(): lax.all_to_all(outgoing, 'replica', split_axis=0, concat_axis=0, tiled=True)  21.7 us
    another operation x1, loops' own time, blockwise_shrink(): lax.scan(one_block, jnp.float32(0.0), (source_row.reshape(block_count, bl...  19.9 us
    all_to_all x1, blocking collectives, shards(): lax.all_to_all(requests.reshape(replicas, 1), 'replica', split_axis=0, co...  18.4 us
    all_to_all x1, starting transfers between devices, shards(): lax.all_to_all(outbound_up, 'replica', split_axis=0, concat_axis=0, tiled...  10.1 us
  transfers between devices with their start and end apart: 3, of which 3 were waited for; matrix products, arithmetic and copies ran while one was open for 5% of the time, Pallas kernels for 0%

commit v1 on v0

v1 whole, which is shorter than its diff:
```python
import functools

import jax
import jax.numpy as jnp
from jax import lax
from jax.experimental import pallas as pl
from jax.experimental.pallas import tpu as pltpu
from jax.sharding import PartitionSpec as P

RINGS = 8
USE = 8
SCALE = 0.5
CHUNKS = 4

BF16 = jnp.bfloat16
F32 = jnp.float32
MESH = pl.DeviceIdType.MESH


def slot_of(d, n):
    d %= n
    return 0 if d == 0 else (2 * d - 1 if d <= n // 2 else 2 * (n - d))


def shift_of(k, n):
    odd = k % 2
    return odd * ((k + 1) // 2) + (1 - odd) * ((n - k // 2) % n)


def kernel(
    dims,
    hid, kvw, down, up, idx, dest,
    out,
    hf, kvb, kvf, base, hbuf, wbuf, upz, colbuf, idz, idy, acc, rs, sh, hm, sr, upsend, upsel, bd, perm, kvs,
    local_sem, z_send, z_recv, w_send, w_recv, u_send, u_recv, i_send, i_recv, j_send, j_recv,
    a_send, a_recv, b_send, b_recv, c_send, c_recv, s_send, s_recv, o_send, o_recv,
):
    nz, ny, nt = dims
    rows, width = hbuf.shape[1], hbuf.shape[2]
    adapters, rank = wbuf.shape[1], wbuf.shape[3]
    sub = rows // nt
    piece = rows // CHUNKS
    cap2 = kvs.shape[1]
    replicas = nz * ny
    hz, hy = nz // 2, ny // 2

    r = lax.axis_index("replica")
    t = lax.axis_index("tensor")
    z, y = r // ny, r % ny

    def at_z(d):
        return ((z + d + nz) % nz) * ny + y

    def at_y(d):
        return z * ny + (y + d + ny) % ny

    def remote(src, dst, send, recv, replica, tensor):
        return pltpu.make_async_remote_copy(
            src_ref=src, dst_ref=dst, send_sem=send, recv_sem=recv,
            device_id=(replica, tensor), device_id_type=MESH,
        )

    own_cols = pl.ds(pl.multiple_of(t * width, 128), width)
    own_h = pltpu.make_async_copy(hid.at[:, own_cols], hbuf.at[0], local_sem.at[0])
    own_w = pltpu.make_async_copy(down, wbuf.at[0], local_sem.at[1])
    own_u = pltpu.make_async_copy(up, upz.at[0], local_sem.at[2])
    own_k = pltpu.make_async_copy(kvw, kvb, local_sem.at[3])

    def full_copy(c):
        return pltpu.make_async_copy(
            hid.at[:, pl.ds(pl.multiple_of(c * width, 128), width)], hf.at[c], local_sem.at[4 + c]
        )

    own_h.start()
    own_w.start()
    own_u.start()
    own_k.start()
    lax.fori_loop(0, nt, lambda c, _: (full_copy(c).start(), 0)[1], 0)

    barrier = pltpu.get_barrier_semaphore()

    def greet_replica(i, _):
        pl.semaphore_signal(
            barrier, inc=1, device_id=((r + i) % replicas, t), device_id_type=MESH
        )
        return 0

    def greet_tensor(i, _):
        pl.semaphore_signal(barrier, inc=1, device_id=(r, (t + i) % nt), device_id_type=MESH)
        return 0

    lax.fori_loop(1, replicas, greet_replica, 0)
    lax.fori_loop(1, nt, greet_tensor, 0)
    pl.semaphore_wait(barrier, replicas - 1 + nt - 1)

    def z_copy(way, step, c):
        part = pl.ds(c * piece, piece)
        sign = -1 if way == 0 else 1
        to = at_z(1 if way == 0 else -1)
        dst = hbuf.at[slot_of(sign * step, nz), part]
        if step == 1:
            src = hid.at[part, own_cols]
        else:
            src = hbuf.at[slot_of(sign * (step - 1), nz), part]
        return remote(src, dst, z_send.at[way, step, c], z_recv.at[way, step, c], to, t)

    def z_takes(way, step, c):
        return step < hz or (step == hz and (c < CHUNKS // 2) == (way == 0))

    def u_copy(way, step):
        sign = -1 if way == 0 else 1
        to = at_z(1 if way == 0 else -1)
        n = upz.shape[1]
        part = pl.ds(0, n) if step < hz else pl.ds(way * (n // 2), n // 2)
        dst = upz.at[slot_of(sign * step, nz), part]
        if step == 1:
            src = up.at[part]
        else:
            src = upz.at[slot_of(sign * (step - 1), nz), part]
        return remote(src, dst, u_send.at[way, step], u_recv.at[way, step], to, t)

    def w_copy(way, step, j):
        sign = -1 if way == 0 else 1
        to = at_y(1 if way == 0 else -1)
        dst = wbuf.at[slot_of(sign * step, ny), j]
        src = down.at[j] if step == 1 else wbuf.at[slot_of(sign * (step - 1), ny), j]
        return remote(src, dst, w_send.at[way, step, j], w_recv.at[way, step, j], to, t)

    def w_takes(way, step, j):
        return step < hy or (step == hy and (j < adapters // 2) == (way == 0))

    def i_copy(d):
        return remote(idx, idz.at[slot_of(-d, nz)], i_send.at[d], i_recv.at[d], at_z(d), t)

    def j_copy(d):
        return remote(idx, idy.at[(-d) % ny], j_send.at[d], j_recv.at[d], at_y(d), t)

    for d in range(1, nz):
        i_copy(d).start()
    for d in range(1, ny):
        j_copy(d).start()
    w_order = [list(range(adapters)), list(range(adapters // 2, adapters)) + list(range(adapters // 2))]
    for c in range(CHUNKS):
        for way in range(2):
            if z_takes(way, 1, c):
                z_copy(way, 1, c).start()
        for way in range(2):
            if c < adapters and w_takes(way, 1, w_order[way][c]):
                w_copy(way, 1, w_order[way][c]).start()
    for way in range(2):
        u_copy(way, 1).start()

    eye = lax.broadcasted_iota(jnp.int32, (rows, rows), 0) == lax.broadcasted_iota(
        jnp.int32, (rows, rows), 1
    )

    def column(row):
        wide = jnp.broadcast_to(row, (rows, rows))
        return jnp.sum(jnp.where(eye, wide, 0.0), axis=1, keepdims=True)

    def base_part(c, _):
        words = 2 * width
        at = pl.ds(pl.multiple_of(c * words, 128), words)
        kvf[...] = kvb[at, :].astype(F32)
        keys = kvf[pl.ds(0, width, stride=2), :].astype(BF16)
        values = kvf[pl.ds(1, width, stride=2), :].astype(BF16)
        both = jnp.concatenate([keys, values], axis=1)
        base[...] += jnp.dot(hf[c], both, preferred_element_type=F32)
        return 0

    def unit(k, m):
        mate = shift_of(m, ny)
        first = (z * ny + (y + mate) % ny) * adapters
        wanted = colbuf[k]
        total = acc[k].reshape(rows, rank)
        h = hbuf[k]
        for pair in range(adapters // 2):
            w = jnp.concatenate([wbuf[m, 2 * pair], wbuf[m, 2 * pair + 1]], axis=1)
            got = jnp.dot(h, w, preferred_element_type=F32)
            for j in range(2):
                mine = wanted == first + 2 * pair + j
                total = total + jnp.where(mine, got[:, j * rank : (j + 1) * rank], 0.0)
        acc[k] = total.reshape(nt, sub, rank)

    def units(k_low, k_high, m_low, m_high):
        count = m_high - m_low

        def one(i, _):
            unit(k_low + i // count, m_low + i % count)
            return 0

        lax.fori_loop(0, (k_high - k_low) * count, one, 0)

    base[...] = jnp.zeros_like(base)
    acc[...] = jnp.zeros_like(acc)
    to_row = dest[...].astype(F32)
    to_col = column(to_row)
    before = lax.broadcasted_iota(jnp.int32, (rows, rows), 0) < lax.broadcasted_iota(
        jnp.int32, (rows, rows), 1
    )
    earlier = jnp.where(before & (to_col == to_row), 1.0, 0.0)
    order = jnp.sum(earlier, axis=0, keepdims=True)
    place = to_row * float(cap2) + order * 2.0
    n_perm = perm.shape[0]
    for p in range(2):
        target = lax.broadcasted_iota(jnp.int32, (n_perm, rows), 0).astype(F32)
        perm[:, p * rows : (p + 1) * rows] = jnp.where(target == place + float(p), 1.0, 0.0).astype(
            BF16
        )

    def wide_column(k, row):
        colbuf[k] = jnp.broadcast_to(column(row.astype(F32)), (rows, rank)).astype(jnp.int32)

    wide_column(0, idx[...])
    own_h.wait()
    own_w.wait()
    own_k.wait()
    lax.fori_loop(0, nt, lambda c, _: (full_copy(c).wait(), 0)[1], 0)
    unit(0, 0)
    for d in range(1, nz):
        i_copy(d).wait_recv()
        k = slot_of(-d, nz)
        wide_column(k, idz[k])

    base_done = 0
    w_step1 = [(way, w_order[way][n]) for n in range(adapters) for way in range(2)]
    w_step1 = [(way, j) for way, j in w_step1 if w_takes(way, 1, j)]
    w_next = 0
    for step in range(1, hz):
        for c in range(CHUNKS):
            for way in range(2):
                z_copy(way, step, c).wait_recv()
                if z_takes(way, step + 1, c):
                    z_copy(way, step + 1, c).start()
            if c % 2 == 1:
                for _ in range(2):
                    if w_next < len(w_step1):
                        way, j = w_step1[w_next]
                        w_copy(way, 1, j).wait_recv()
                        if hy > 1 and w_takes(way, 2, j):
                            w_copy(way, 2, j).start()
                        w_next += 1
            if base_done < nt:
                more = min(2, nt - base_done)
                lax.fori_loop(base_done, base_done + more, base_part, 0)
                base_done += more
        for way in range(2):
            u_copy(way, step).wait_recv()
            u_copy(way, step + 1).start()
        if step == 1:
            units(1, 3, 0, 1)
        elif step == 2:
            units(3, 5, 0, 1)
    for way, j in w_step1[w_next:]:
        w_copy(way, 1, j).wait_recv()
        if hy > 1 and w_takes(way, 2, j):
            w_copy(way, 2, j).start()
    if base_done < nt:
        lax.fori_loop(base_done, nt, base_part, 0)
    early = min(nz - 1, 5)
    if hy > 1:
        units(0, early, 1, 3)
        for j in range(adapters):
            w_copy(0 if j < adapters // 2 else 1, 2, j).wait_recv()
    units(0, early, ny - 1, ny)
    if early < nz - 1:
        units(early, nz - 1, 0, ny)

    def a_copy(i, part, low, count):
        to = (t + i) % nt
        span = pl.ds(low, count)
        return remote(
            acc.at[span, to], rs.at[i, span], a_send.at[part, i], a_recv.at[part, i], r, to
        )

    def start_a(part, low, count):
        lax.fori_loop(1, nt, lambda i, _: (a_copy(i, part, low, count).start(), 0)[1], 0)

    def finish_a(part, low, count):
        lax.fori_loop(1, nt, lambda i, _: (a_copy(i, part, low, count).wait_recv(), 0)[1], 0)
        total = acc[low : low + count, t]
        for i in range(1, nt):
            total = total + rs[i, low : low + count]
        sh[low : low + count] = total.astype(BF16)

    def b_copy(k):
        d = 0 if k == 0 else next(d for d in range(1, nz) if slot_of(d, nz) == k)
        return remote(
            sh.at[k], hm.at[slot_of(-d, nz)], b_send.at[k], b_recv.at[slot_of(-d, nz)], at_z(d), t
        )

    start_a(0, 0, nz - 1)

    for way in range(2):
        u_copy(way, hz).wait_recv()
    own_u.wait()
    for d in range(1, ny):
        j_copy(d).wait_recv()

    def select_up(wanted, into):
        def one(k, _):
            first = (((z + shift_of(k, nz)) % nz) * ny + y) * adapters
            total = jnp.zeros((rank, 128), F32)
            for j in range(adapters):
                uses = jnp.where(wanted == first + j, 1.0, 0.0)
                uses = jnp.max(uses, axis=1, keepdims=True)
                total = total + uses * upz[k, j * rank : (j + 1) * rank].astype(F32)
            into[k] = total.astype(BF16)
            return 0

        lax.fori_loop(0, nz, one, 0)

    def s_copy(d):
        return remote(
            upsend.at[d], upsel.at[(-d) % ny], s_send.at[d], s_recv.at[d], at_y(d), t
        )

    for d in range(1, ny):
        select_up(idy[d], upsend.at[d])
        s_copy(d).start()
    select_up(idx[...], upsel.at[0])

    finish_a(0, 0, nz - 1)
    hm[0] = sh[0]
    for k in range(1, nz - 1):
        b_copy(k).start()
    for c in range(CHUNKS):
        way = 0 if c < CHUNKS // 2 else 1
        z_copy(way, hz, c).wait_recv()
    units(nz - 1, nz, 0, ny)
    start_a(1, nz - 1, 1)

    rank_half = (lax.broadcasted_iota(jnp.int32, (rank, 128), 0) < rank // 2).astype(F32)

    def spread_up(e):
        def one(k, _):
            block = upsel[e, k].astype(F32)
            bd[e, pl.ds(pl.multiple_of(k * rank, rank), rank), 0:128] = (block * rank_half).astype(BF16)
            bd[e, pl.ds(pl.multiple_of(k * rank, rank), rank), 128:256] = (
                block * (1.0 - rank_half)
            ).astype(BF16)
            return 0

        lax.fori_loop(0, nz, one, 0)

    spread_up(0)
    finish_a(1, nz - 1, 1)
    b_copy(nz - 1).start()
    for d in range(1, ny):
        s_copy(d).wait_recv()
        spread_up(ny - d)

    for k in range(1, nz):
        b_copy(k).wait_recv()
    mine = hm[0].astype(F32)
    for k in range(1, nz):
        mine = mine + hm[k].astype(F32)
    sr[t] = mine.astype(BF16)

    def c_copy(i):
        return remote(sr.at[t], sr.at[t], c_send.at[i], c_recv.at[i], r, (t + i) % nt)

    def c_arrival(i):
        src = (t + nt - i) % nt
        return remote(sr.at[src], sr.at[src], c_send.at[i], c_recv.at[i], r, src)

    lax.fori_loop(1, nt, lambda i, _: (c_copy(i).start(), 0)[1], 0)
    lax.fori_loop(1, nt, lambda i, _: (c_arrival(i).wait_recv(), 0)[1], 0)

    shrink = sr[...].astype(F32).reshape(rows, rank)
    wanted = colbuf[0]

    def delta_part(e, _):
        parts = []
        for k in range(nz):
            d = shift_of(k, nz)
            first = (((z + d) % nz) * ny + (y + e) % ny) * adapters
            uses = (wanted >= first) & (wanted < first + adapters)
            parts.append(jnp.where(uses, shrink, 0.0).astype(BF16))
        spread = jnp.concatenate(parts, axis=1)
        base[...] += SCALE * jnp.dot(spread, bd[e], preferred_element_type=F32)
        return 0

    lax.fori_loop(0, ny, delta_part, 0)
    projected = base[...].astype(BF16)
    stacked = jnp.concatenate([projected[:, 0:128], projected[:, 128:256]], axis=0)
    cache = jnp.dot(perm[...], stacked, preferred_element_type=F32).astype(BF16)
    kvs[...] = cache.reshape(replicas, cap2, 128)

    def o_copy(i):
        to = (r + i) % replicas
        return remote(
            kvs.at[to], out.at[pl.ds(pl.multiple_of(r * cap2, cap2), cap2)],
            o_send.at[i], o_recv.at[i], to, t,
        )

    def o_arrival(i):
        src = (r + replicas - i) % replicas
        return remote(
            kvs.at[src], out.at[pl.ds(pl.multiple_of(src * cap2, cap2), cap2)],
            o_send.at[i], o_recv.at[i], src, t,
        )

    lax.fori_loop(1, replicas, lambda i, _: (o_copy(i).start(), 0)[1], 0)
    own_o = pltpu.make_async_copy(
        kvs.at[r], out.at[pl.ds(pl.multiple_of(r * cap2, cap2), cap2)], local_sem.at[4 + nt]
    )
    own_o.start()

    for way in range(2):
        for step in range(1, hz + 1):
            for c in range(CHUNKS):
                if z_takes(way, step, c):
                    z_copy(way, step, c).wait_send()
            u_copy(way, step).wait_send()
        for step in range(1, hy + 1):
            for j in range(adapters):
                if w_takes(way, step, j):
                    w_copy(way, step, j).wait_send()
    for d in range(1, nz):
        i_copy(d).wait_send()
    for d in range(1, ny):
        j_copy(d).wait_send()
        s_copy(d).wait_send()
    for k in range(1, nz):
        b_copy(k).wait_send()

    def tensor_sends(i, _):
        a_copy(i, 0, 0, nz - 1).wait_send()
        a_copy(i, 1, nz - 1, 1).wait_send()
        c_copy(i).wait_send()
        return 0

    lax.fori_loop(1, nt, tensor_sends, 0)

    def last(i, _):
        o_copy(i).wait_send()
        o_arrival(i).wait_recv()
        return 0

    lax.fori_loop(1, replicas, last, 0)
    own_o.wait()


def shards(nz, hidden, key_value_weight, adapter_down_weight, adapter_up_weight, token_adapter_index, destinations):
    replicas = lax.axis_size("replica")
    nt = lax.axis_size("tensor")
    ny = replicas // nz
    rows, model = hidden.shape
    width = model // nt
    adapters, _, rank = adapter_down_weight.shape
    cols = key_value_weight.shape[2]
    cap2 = 2 * (2 * rows // replicas)
    sub = rows // nt
    hz, hy = nz // 2, ny // 2
    vm = pltpu.VMEM
    dma = pltpu.SemaphoreType.DMA
    scratch = [
        vm((nt, rows, width), BF16),
        vm((2 * model, cols), BF16),
        vm((2 * width, cols), F32),
        vm((rows, 2 * cols), F32),
        vm((nz, rows, width), BF16),
        vm((ny, adapters, width, rank), BF16),
        vm((nz, adapters * rank, cols), BF16),
        vm((nz, rows, rank), jnp.int32),
        vm((nz, 1, rows), jnp.int32),
        vm((ny, 1, rows), jnp.int32),
        vm((nz, nt, sub, rank), F32),
        vm((nt, nz, sub, rank), F32),
        vm((nz, sub, rank), BF16),
        vm((nz, sub, rank), BF16),
        vm((nt, sub, rank), BF16),
        vm((ny, nz, rank, cols), BF16),
        vm((ny, nz, rank, cols), BF16),
        vm((ny, nz * rank, 2 * cols), BF16),
        vm((replicas * cap2, 2 * rows), BF16),
        vm((replicas, cap2, cols), BF16),
        dma((5 + nt,)),
        dma((2, hz + 1, CHUNKS)), dma((2, hz + 1, CHUNKS)),
        dma((2, hy + 1, adapters)), dma((2, hy + 1, adapters)),
        dma((2, hz + 1)), dma((2, hz + 1)),
        dma((nz,)), dma((nz,)),
        dma((ny,)), dma((ny,)),
        dma((2, nt)), dma((2, nt)),
        dma((nz,)), dma((nz,)),
        dma((nt,)), dma((nt,)),
        dma((ny,)), dma((ny,)),
        dma((replicas,)), dma((replicas,)),
    ]
    hbm = pl.BlockSpec(memory_space=pltpu.HBM)
    in_vmem = pl.BlockSpec(memory_space=pltpu.VMEM)
    cache = pl.pallas_call(
        functools.partial(kernel, (nz, ny, nt)),
        out_shape=jax.ShapeDtypeStruct((replicas * cap2, cols), BF16),
        in_specs=[hbm, hbm, hbm, hbm, in_vmem, in_vmem],
        out_specs=hbm,
        scratch_shapes=scratch,
        compiler_params=pltpu.CompilerParams(
            collective_id=0, has_side_effects=True, vmem_limit_bytes=56 * 1024 * 1024
        ),
        cost_estimate=pl.CostEstimate(
            flops=2 * rows * model * 2 * cols + 2 * nz * rows * width * ny * adapters * rank,
            bytes_accessed=2 * (rows * model + 2 * model * cols + adapters * width * rank),
            transcendentals=0,
        ),
    )(
        hidden,
        key_value_weight.reshape(2 * model, cols),
        adapter_down_weight,
        adapter_up_weight.reshape(adapters * rank, cols),
        token_adapter_index.reshape(1, rows),
        destinations.reshape(1, rows),
    )
    return cache.reshape(replicas * cap2 // 2, 2, cols)


def solution(mesh):
    placed = (
        P("replica", None),
        P(None, None, "tensor"),
        P("replica", "tensor", None),
        P("replica", None, None, "tensor"),
        P("replica"),
        P("replica", None),
    )
    return jax.shard_map(
        functools.partial(shards, RINGS), mesh=mesh, in_specs=placed,
        out_specs=P("replica", None, "tensor"), check_vma=False,
    )
```

time: 500 us -> 106 us (0.21)
  waiting for transfers between devices: 240 us -> 0 us
  local copies, waits for them, and re-layouts: 118 us -> 1.83 us
  Pallas kernels: 0 us -> 104 us
  blocking collectives: 40.1 us -> 0 us
  matrix products: 31.5 us -> 0 us
  loops' own time: 19.9 us -> 0 us
  starting transfers between devices: 16.9 us -> 0 us
  other arithmetic: 16 us -> 0 us
  between operations: 13.7 us -> 0.01 us
    all_to_all x2 -> x0, waiting for transfers between devices: 193 us -> none  [the longest x1 185 us: shards(): lax.all_to_all(outbound_down, 'replica', split_axis=0, concat_axis=0, til...]
    pallas_call x0 -> x1, Pallas kernels: none -> 104 us  [shards(): pl.pallas_call(functools.partial(kernel, (nz, ny, nt)), out_shape=jax.Sha...]
    gather x16 -> x0, local copies, waits for them, and re-layouts: 77.5 us -> none  [the longest x10 65.4 us: one_block(): rows = jnp.take(source_hidden, row_ids, axis=0)]
    all_gather x1 -> x0, waiting for transfers between devices: 46.8 us -> none  [shards(): whole_down = lax.all_gather(fetched_down, 'tensor', axis=1, tiled=True)]
    all_to_all x2 -> x0, blocking collectives: 40.1 us -> none  [the longest x1 21.7 us: shards(): lax.all_to_all(outgoing, 'replica', split_axis=0, concat_axis=0, tiled=True)]
    dot_general x12 -> x0, matrix products: 31.5 us -> none  [the longest x10 26.3 us: one_block(): jnp.dot(rows, weight, preferred_element_type=jnp.float32)]
    another operation x1 -> x0, loops' own time: 19.9 us -> none  [blockwise_shrink(): lax.scan(one_block, jnp.float32(0.0), (source_row.reshape(block_count, bl...]
    all_to_all x2 -> x0, starting transfers between devices: 16.9 us -> none  [the longest x1 10.1 us: shards(): lax.all_to_all(outbound_up, 'replica', split_axis=0, concat_axis=0, tiled...]
  transfers between devices with their start and end apart: 3 -> 0, of which waited for: 3 -> 0; matrix products, arithmetic and copies ran while one was open for 5% -> 0% of each run, Pallas kernels for 0% -> 0%
where the time goes in v1:
time: 106 us
  Pallas kernels  104 us (98%)
  local copies, waits for them, and re-layouts  1.83 us (2%)
    pallas_call x1, Pallas kernels, shards(): pl.pallas_call(functools.partial(kernel, (nz, ny, nt)), out_shape=jax.Sha...  104 us

profile of v1, /device:TPU:64, one launch (start us, length us, event | category | flops | bytes accessed | tf_op | source)
XLA Modules:
  0.0 106.1 jit_solution(16839764465609870826)
XLA Ops:
  0.0 104.3 %shard_map.64 = bf16[1024,128]{1,0:T(8,128)(2,1)} custom-call(bf16[256,8192]{1,0:T(8,128)(2,1)} %hid.1, bf16[16384,128]{1,0:T(8,128)(2,1)} %bitcast.6, bf16[4,1024,128]{2,1,0:T(8,128)(2,1)} %down.1, bf16[512,128]{1,0:T(8,128)(2,1)} %bitcast.7, s32[1,256]{1,0:T(1,128)} %bitcast.8, s32[1,256]{1,0:T(1,128)} %bitcast.9), custom_call_target="tpu_custom_call" | custom-call | flops 9663676416 | bytes 9437184 | tf_op jit(solution)/shard_map/pallas_call | solution.py:493
  104.3 1.8 %copy.8 = bf16[512,2,128]{2,1,0:T(2,128)(2,1)} copy(bf16[512,2,128]{2,1,0:T(2,128)(2,1)} %bitcast.5) | data formatting | bytes 524288

commit v2 on v1

--- a/solution.py
+++ b/solution.py
@@ -31,9 +31,9 @@
     dims,
     hid, kvw, down, up, idx, dest,
     out,
-    hf, kvb, kvf, base, hbuf, wbuf, upz, colbuf, idz, idy, acc, rs, sh, hm, sr, upsend, upsel, bd, perm, kvs,
+    hf, kvb, kvf, base, hbuf, wbuf, upz, colbuf, idz, idy, acc, halves, part, rs, sh, hm, sr, upsend, upsel, bd, perm, kvs,
     local_sem, z_send, z_recv, w_send, w_recv, u_send, u_recv, i_send, i_recv, j_send, j_recv,
-    a_send, a_recv, b_send, b_recv, c_send, c_recv, s_send, s_recv, o_send, o_recv,
+    p_send, p_recv, a_send, a_recv, b_send, b_recv, c_send, c_recv, s_send, s_recv, o_send, o_recv,
 ):
     nz, ny, nt = dims
     rows, width = hbuf.shape[1], hbuf.shape[2]
@@ -47,6 +47,9 @@
     r = lax.axis_index("replica")
     t = lax.axis_index("tensor")
     z, y = r // ny, r % ny
+    nx = nt // 2
+    x, core = t // 2, t % 2
+    share = core * nx + x
 
     def at_z(d):
         return ((z + d + nz) % nz) * ny + y
@@ -79,19 +82,14 @@
 
     barrier = pltpu.get_barrier_semaphore()
 
-    def greet_replica(i, _):
-        pl.semaphore_signal(
-            barrier, inc=1, device_id=((r + i) % replicas, t), device_id_type=MESH
-        )
-        return 0
-
     def greet_tensor(i, _):
         pl.semaphore_signal(barrier, inc=1, device_id=(r, (t + i) % nt), device_id_type=MESH)
         return 0
 
-    lax.fori_loop(1, replicas, greet_replica, 0)
+    for to in (at_z(1), at_z(-1), at_y(1), at_y(-1)):
+        pl.semaphore_signal(barrier, inc=1, device_id=(to, t), device_id_type=MESH)
     lax.fori_loop(1, nt, greet_tensor, 0)
-    pl.semaphore_wait(barrier, replicas - 1 + nt - 1)
+    pl.semaphore_wait(barrier, 4 + nt - 1)
 
     def z_copy(way, step, c):
         part = pl.ds(c * piece, piece)
@@ -107,17 +105,26 @@
     def z_takes(way, step, c):
         return step < hz or (step == hz and (c < CHUNKS // 2) == (way == 0))
 
-    def u_copy(way, step):
+    def u_copy(way, step, h):
         sign = -1 if way == 0 else 1
         to = at_z(1 if way == 0 else -1)
-        n = upz.shape[1]
-        part = pl.ds(0, n) if step < hz else pl.ds(way * (n // 2), n // 2)
+        n = upz.shape[1] // 2
+        part = pl.ds(h * n, n)
         dst = upz.at[slot_of(sign * step, nz), part]
         if step == 1:
             src = up.at[part]
         else:
             src = upz.at[slot_of(sign * (step - 1), nz), part]
-        return remote(src, dst, u_send.at[way, step], u_recv.at[way, step], to, t)
+        return remote(src, dst, u_send.at[way, step, h], u_recv.at[way, step, h], to, t)
+
+    def u_takes(way, step, h):
+        return step < hz or (step == hz and h == way)
+
+    def u_start():
+        for h in range(2):
+            for way in range(2):
+                if u_takes(way, 1, h):
+                    u_copy(way, 1, h).start()
 
     def w_copy(way, step, j):
         sign = -1 if way == 0 else 1
@@ -129,16 +136,28 @@
     def w_takes(way, step, j):
         return step < hy or (step == hy and (j < adapters // 2) == (way == 0))
 
-    def i_copy(d):
-        return remote(idx, idz.at[slot_of(-d, nz)], i_send.at[d], i_recv.at[d], at_z(d), t)
-
-    def j_copy(d):
-        return remote(idx, idy.at[(-d) % ny], j_send.at[d], j_recv.at[d], at_y(d), t)
-
-    for d in range(1, nz):
-        i_copy(d).start()
-    for d in range(1, ny):
-        j_copy(d).start()
+    def i_copy(way, step):
+        sign = -1 if way == 0 else 1
+        src = idx if step == 1 else idz.at[slot_of(sign * (step - 1), nz)]
+        dst = idz.at[slot_of(sign * step, nz)]
+        to = at_z(1 if way == 0 else -1)
+        return remote(src, dst, i_send.at[way, step], i_recv.at[way, step], to, t)
+
+    def j_copy(way, step):
+        sign = -1 if way == 0 else 1
+        src = idx if step == 1 else idy.at[(sign * (step - 1)) % ny]
+        dst = idy.at[(sign * step) % ny]
+        to = at_y(1 if way == 0 else -1)
+        return remote(src, dst, j_send.at[way, step], j_recv.at[way, step], to, t)
+
+    def once(way, step, half_way):
+        return step < half_way or (step == half_way and way == 0)
+
+    for way in range(2):
+        if once(way, 1, hz):
+            i_copy(way, 1).start()
+        if once(way, 1, hy):
+            j_copy(way, 1).start()
     w_order = [list(range(adapters)), list(range(adapters // 2, adapters)) + list(range(adapters // 2))]
     for c in range(CHUNKS):
         for way in range(2):
@@ -147,8 +166,7 @@
         for way in range(2):
             if c < adapters and w_takes(way, 1, w_order[way][c]):
                 w_copy(way, 1, w_order[way][c]).start()
-    for way in range(2):
-        u_copy(way, 1).start()
+    u_start()
 
     eye = lax.broadcasted_iota(jnp.int32, (rows, rows), 0) == lax.broadcasted_iota(
         jnp.int32, (rows, rows), 1
@@ -180,7 +198,7 @@
             for j in range(2):
                 mine = wanted == first + 2 * pair + j
                 total = total + jnp.where(mine, got[:, j * rank : (j + 1) * rank], 0.0)
-        acc[k] = total.reshape(nt, sub, rank)
+        acc[k] = total.reshape(2, nx, sub, rank)
 
     def units(k_low, k_high, m_low, m_high):
         count = m_high - m_low
@@ -189,7 +207,10 @@
             unit(k_low + i // count, m_low + i % count)
             return 0
 
-        lax.fori_loop(0, (k_high - k_low) * count, one, 0)
+        if (k_high - k_low) * count == 1:
+            unit(k_low, m_low)
+        else:
+            lax.fori_loop(0, (k_high - k_low) * count, one, 0)
 
     base[...] = jnp.zeros_like(base)
     acc[...] = jnp.zeros_like(acc)
@@ -216,16 +237,54 @@
     own_w.wait()
     own_k.wait()
     lax.fori_loop(0, nt, lambda c, _: (full_copy(c).wait(), 0)[1], 0)
-    unit(0, 0)
-    for d in range(1, nz):
-        i_copy(d).wait_recv()
-        k = slot_of(-d, nz)
-        wide_column(k, idz[k])
-
-    base_done = 0
-    w_step1 = [(way, w_order[way][n]) for n in range(adapters) for way in range(2)]
-    w_step1 = [(way, j) for way, j in w_step1 if w_takes(way, 1, j)]
-    w_next = 0
+
+    groups = [(0, 1)] + [(2 * s - 1, 2 * s + 1) for s in range(1, hz)] + [(nz - 1, nz)]
+    state = {"base": 0, "w": 0}
+    here_k, here_m = {0}, {0}
+    pending = {(k, m) for k in range(nz) for m in range(ny)}
+    w_waits = [
+        [(way, 1, w_order[way][n]) for way in range(2) if w_takes(way, 1, w_order[way][n])]
+        for n in range(adapters)
+    ]
+    if hy > 1:
+        half = adapters // 2
+        w_waits += [[(way, 2, w_order[way][n]) for way in range(2)] for n in range(half)]
+    w_waits = [pair for pair in w_waits if pair]
+
+    def some_units(budget):
+        while budget > 0:
+            ready = sorted((m, k) for k, m in pending if k in here_k and m in here_m)
+            if not ready:
+                return
+            m, low = ready[0]
+            high = low
+            while (m, high) in ready and high - low < budget:
+                pending.discard((high, m))
+                high += 1
+            units(low, high, m, m + 1)
+            budget -= high - low
+
+    def next_w():
+        if state["w"] == len(w_waits):
+            return
+        for way, step, j in w_waits[state["w"]]:
+            w_copy(way, step, j).wait_recv()
+            if step < hy and w_takes(way, step + 1, j):
+                w_copy(way, step + 1, j).start()
+        state["w"] += 1
+        if state["w"] == len(w_waits):
+            here_m.update(range(ny))
+        elif hy > 1 and state["w"] == adapters:
+            here_m.update((1, 2))
+
+    def some_base(count):
+        low = state["base"]
+        high = min(nt, low + count)
+        if low < high:
+            lax.fori_loop(low, high, base_part, 0)
+        state["base"] = high
+        return high - low
+
     for step in range(1, hz):
         for c in range(CHUNKS):
             for way in range(2):
@@ -233,55 +292,53 @@
                 if z_takes(way, step + 1, c):
                     z_copy(way, step + 1, c).start()
             if c % 2 == 1:
-                for _ in range(2):
-                    if w_next < len(w_step1):
-                        way, j = w_step1[w_next]
-                        w_copy(way, 1, j).wait_recv()
-                        if hy > 1 and w_takes(way, 2, j):
-                            w_copy(way, 2, j).start()
-                        w_next += 1
-            if base_done < nt:
-                more = min(2, nt - base_done)
-                lax.fori_loop(base_done, base_done + more, base_part, 0)
-                base_done += more
-        for way in range(2):
-            u_copy(way, step).wait_recv()
-            u_copy(way, step + 1).start()
-        if step == 1:
-            units(1, 3, 0, 1)
-        elif step == 2:
-            units(3, 5, 0, 1)
-    for way, j in w_step1[w_next:]:
-        w_copy(way, 1, j).wait_recv()
-        if hy > 1 and w_takes(way, 2, j):
-            w_copy(way, 2, j).start()
-    if base_done < nt:
-        lax.fori_loop(base_done, nt, base_part, 0)
-    early = min(nz - 1, 5)
-    if hy > 1:
-        units(0, early, 1, 3)
-        for j in range(adapters):
-            w_copy(0 if j < adapters // 2 else 1, 2, j).wait_recv()
-    units(0, early, ny - 1, ny)
-    if early < nz - 1:
-        units(early, nz - 1, 0, ny)
-
-    def a_copy(i, part, low, count):
-        to = (t + i) % nt
-        span = pl.ds(low, count)
+                next_w()
+            if c == CHUNKS - 1:
+                for way in range(2):
+                    k = slot_of(-step if way == 0 else step, nz)
+                    wide_column(k, idz[k])
+                    here_k.add(k)
+            if c == 0:
+                for way in range(2):
+                    i_copy(way, step).wait_recv()
+                    if once(way, step + 1, hz):
+                        i_copy(way, step + 1).start()
+                    if step < hy:
+                        j_copy(way, step).wait_recv()
+                        if once(way, step + 1, hy):
+                            j_copy(way, step + 1).start()
+            if not some_base(3):
+                some_units(4)
+    while state["w"] < len(w_waits):
+        next_w()
+    some_base(nt)
+
+    def p_copy(g):
+        span = pl.ds(groups[g][0], groups[g][1] - groups[g][0])
         return remote(
-            acc.at[span, to], rs.at[i, span], a_send.at[part, i], a_recv.at[part, i], r, to
-        )
-
-    def start_a(part, low, count):
-        lax.fori_loop(1, nt, lambda i, _: (a_copy(i, part, low, count).start(), 0)[1], 0)
-
-    def finish_a(part, low, count):
-        lax.fori_loop(1, nt, lambda i, _: (a_copy(i, part, low, count).wait_recv(), 0)[1], 0)
-        total = acc[low : low + count, t]
-        for i in range(1, nt):
-            total = total + rs[i, low : low + count]
-        sh[low : low + count] = total.astype(BF16)
+            acc.at[span, 1 - core], halves.at[span], p_send.at[g], p_recv.at[g], r, t + 1 - 2 * core
+        )
+
+    def a_copy(i, g):
+        to = (x + i) % nx
+        span = pl.ds(groups[g][0], groups[g][1] - groups[g][0])
+        return remote(
+            part.at[span, to], rs.at[i, span], a_send.at[g, i], a_recv.at[g, i], r, 2 * to + core
+        )
+
+    def pass_on(g):
+        low, high = groups[g]
+        p_copy(g).wait_recv()
+        part[low:high] = acc[low:high, core] + halves[low:high]
+        lax.fori_loop(1, nx, lambda i, _: (a_copy(i, g).start(), 0)[1], 0)
+
+    def finish_a(g):
+        low, high = groups[g]
+        lax.fori_loop(1, nx, lambda i, _: (a_copy(i, g).wait_recv(), 0)[1], 0)
+        total = part[low:high, x]
+        for i in range(1, nx):
+            total = total + rs[i, low:high]
+        sh[low:high] = total.astype(BF16)
 
     def b_copy(k):
         d = 0 if k == 0 else next(d for d in range(1, nz) if slot_of(d, nz) == k)
@@ -289,15 +346,30 @@
             sh.at[k], hm.at[slot_of(-d, nz)], b_send.at[k], b_recv.at[slot_of(-d, nz)], at_z(d), t
         )
 
-    start_a(0, 0, nz - 1)
-
-    for way in range(2):
-        u_copy(way, hz).wait_recv()
-    own_u.wait()
-    for d in range(1, ny):
-        j_copy(d).wait_recv()
-
-    def select_up(wanted, into):
+    def finish(g):
+        low, high = groups[g]
+        finish_a(g)
+        for k in range(low, high):
+            if k == 0:
+                hm[0] = sh[0]
+            else:
+                b_copy(k).start()
+
+    def rest_of(g):
+        low, high = groups[g]
+        for k in range(low, high):
+            ms = [m for m in range(ny) if (k, m) in pending]
+            mates = [n for n in range(k, high) if [m for m in range(ny) if (n, m) in pending] == ms]
+            if ms and mates == list(range(k, k + len(mates))) and ms == list(range(ms[0], ny)):
+                units(k, k + len(mates), ms[0], ny)
+                pending.difference_update((n, m) for n in mates for m in ms)
+            else:
+                for m in ms:
+                    units(k, k + 1, m, m + 1)
+                    pending.discard((k, m))
+        p_copy(g).start()
+
+    def select_up(wanted, into, low, high):
         def one(k, _):
             first = (((z + shift_of(k, nz)) % nz) * ny + y) * adapters
             total = jnp.zeros((rank, 128), F32)
@@ -308,63 +380,101 @@
             into[k] = total.astype(BF16)
             return 0
 
-        lax.fori_loop(0, nz, one, 0)
-
-    def s_copy(d):
+        lax.fori_loop(low, high, one, 0)
+
+    u_groups = groups
+
+    def s_copy(d, g):
+        span = pl.ds(u_groups[g][0], u_groups[g][1] - u_groups[g][0])
         return remote(
-            upsend.at[d], upsel.at[(-d) % ny], s_send.at[d], s_recv.at[d], at_y(d), t
-        )
-
-    for d in range(1, ny):
-        select_up(idy[d], upsend.at[d])
-        s_copy(d).start()
-    select_up(idx[...], upsel.at[0])
-
-    finish_a(0, 0, nz - 1)
-    hm[0] = sh[0]
-    for k in range(1, nz - 1):
-        b_copy(k).start()
-    for c in range(CHUNKS):
-        way = 0 if c < CHUNKS // 2 else 1
-        z_copy(way, hz, c).wait_recv()
-    units(nz - 1, nz, 0, ny)
-    start_a(1, nz - 1, 1)
+            upsend.at[d, span], upsel.at[(-d) % ny, span], s_send.at[d, g], s_recv.at[d, g], at_y(d), t
+        )
 
     rank_half = (lax.broadcasted_iota(jnp.int32, (rank, 128), 0) < rank // 2).astype(F32)
 
-    def spread_up(e):
+    def spread_up(e, g):
         def one(k, _):
             block = upsel[e, k].astype(F32)
-            bd[e, pl.ds(pl.multiple_of(k * rank, rank), rank), 0:128] = (block * rank_half).astype(BF16)
-            bd[e, pl.ds(pl.multiple_of(k * rank, rank), rank), 128:256] = (
-                block * (1.0 - rank_half)
-            ).astype(BF16)
+            at = pl.ds(pl.multiple_of(k * rank, rank), rank)
+            bd[e, at, 0:128] = (block * rank_half).astype(BF16)
+            bd[e, at, 128:256] = (block * (1.0 - rank_half)).astype(BF16)
             return 0
 
-        lax.fori_loop(0, nz, one, 0)
-
-    spread_up(0)
-    finish_a(1, nz - 1, 1)
-    b_copy(nz - 1).start()
-    for d in range(1, ny):
-        s_copy(d).wait_recv()
-        spread_up(ny - d)
+        lax.fori_loop(u_groups[g][0], u_groups[g][1], one, 0)
+
+    def u_pass(step):
+        for h in range(2):
+            for way in range(2):
+                if u_takes(way, step, h):
+                    u_copy(way, step, h).wait_recv()
+                    if u_takes(way, step + 1, h):
+                        u_copy(way, step + 1, h).start()
+
+    def u_group(g):
+        for d in range(1, ny):
+            select_up(idy[d], upsend.at[d], *u_groups[g])
+            s_copy(d, g).start()
+        select_up(idx[...], upsel.at[0], *u_groups[g])
+        spread_up(0, g)
+
+    def s_finish(g):
+        for d in range(1, ny):
+            s_copy(d, g).wait_recv()
+            spread_up(ny - d, g)
+
+    for step in range(hz, hy):
+        for way in range(2):
+            j_copy(way, step).wait_recv()
+            if once(way, step + 1, hy):
+                j_copy(way, step + 1).start()
+    j_copy(0, hy).wait_recv()
+    own_u.wait()
+    u_group(0)
+    last = len(groups) - 1
+    for g in range(last):
+        rest_of(g)
+        if g:
+            pass_on(g - 1)
+    for c in range(CHUNKS // 2):
+        z_copy(0, hz, c).wait_recv()
+        z_copy(1, hz, c + CHUNKS // 2).wait_recv()
+        if c == 0:
+            u_pass(1)
+            pass_on(last - 1)
+            u_group(1)
+    i_copy(0, hz).wait_recv()
+    wide_column(nz - 1, idz[nz - 1])
+    rest_of(last)
+    for g in range(last):
+        finish(g)
+    pass_on(last)
+    if hz > 1:
+        u_pass(2)
+    finish(last)
+    for step in range(2, hz):
+        u_group(step)
+        u_pass(step + 1)
+    if hz > 1:
+        u_group(hz)
 
     for k in range(1, nz):
         b_copy(k).wait_recv()
     mine = hm[0].astype(F32)
     for k in range(1, nz):
         mine = mine + hm[k].astype(F32)
-    sr[t] = mine.astype(BF16)
+    sr[share] = mine.astype(BF16)
 
     def c_copy(i):
-        return remote(sr.at[t], sr.at[t], c_send.at[i], c_recv.at[i], r, (t + i) % nt)
+        return remote(sr.at[share], sr.at[share], c_send.at[i], c_recv.at[i], r, (t + i) % nt)
 
     def c_arrival(i):
         src = (t + nt - i) % nt
-        return remote(sr.at[src], sr.at[src], c_send.at[i], c_recv.at[i], r, src)
+        at = (src % 2) * nx + src // 2
+        return remote(sr.at[at], sr.at[at], c_send.at[i], c_recv.at[i], r, src)
 
     lax.fori_loop(1, nt, lambda i, _: (c_copy(i).start(), 0)[1], 0)
+    for g in range(hz + 1):
+        s_finish(g)
     lax.fori_loop(1, nt, lambda i, _: (c_arrival(i).wait_recv(), 0)[1], 0)
 
     shrink = sr[...].astype(F32).reshape(rows, rank)
@@ -412,33 +522,38 @@
             for c in range(CHUNKS):
                 if z_takes(way, step, c):
                     z_copy(way, step, c).wait_send()
-            u_copy(way, step).wait_send()
+            if once(way, step, hz):
+                i_copy(way, step).wait_send()
+            for h in range(2):
+                if u_takes(way, step, h):
+                    u_copy(way, step, h).wait_send()
         for step in range(1, hy + 1):
             for j in range(adapters):
                 if w_takes(way, step, j):
                     w_copy(way, step, j).wait_send()
-    for d in range(1, nz):
-        i_copy(d).wait_send()
+            if once(way, step, hy):
+                j_copy(way, step).wait_send()
     for d in range(1, ny):
-        j_copy(d).wait_send()
-        s_copy(d).wait_send()
+        for g in range(hz + 1):
+            s_copy(d, g).wait_send()
     for k in range(1, nz):
         b_copy(k).wait_send()
 
     def tensor_sends(i, _):
-        a_copy(i, 0, 0, nz - 1).wait_send()
-        a_copy(i, 1, nz - 1, 1).wait_send()
         c_copy(i).wait_send()
         return 0
 
     lax.fori_loop(1, nt, tensor_sends, 0)
-
-    def last(i, _):
+    for g in range(len(groups)):
+        p_copy(g).wait_send()
+        lax.fori_loop(1, nx, lambda i, _, g=g: (a_copy(i, g).wait_send(), 0)[1], 0)
+
+    def cache_rows(i, _):
         o_copy(i).wait_send()
         o_arrival(i).wait_recv()
         return 0
 
-    lax.fori_loop(1, replicas, last, 0)
+    lax.fori_loop(1, replicas, cache_rows, 0)
     own_o.wait()
 
 
@@ -466,8 +581,10 @@
         vm((nz, rows, rank), jnp.int32),
         vm((nz, 1, rows), jnp.int32),
         vm((ny, 1, rows), jnp.int32),
-        vm((nz, nt, sub, rank), F32),
-        vm((nt, nz, sub, rank), F32),
+        vm((nz, 2, nt // 2, sub, rank), F32),
+        vm((nz, nt // 2, sub, rank), F32),
+        vm((nz, nt // 2, sub, rank), F32),
+        vm((nt // 2, nz, sub, rank), F32),
         vm((nz, sub, rank), BF16),
         vm((nz, sub, rank), BF16),
         vm((nt, sub, rank), BF16),
@@ -479,13 +596,14 @@
         dma((5 + nt,)),
         dma((2, hz + 1, CHUNKS)), dma((2, hz + 1, CHUNKS)),
         dma((2, hy + 1, adapters)), dma((2, hy + 1, adapters)),
+        dma((2, hz + 1, 2)), dma((2, hz + 1, 2)),
         dma((2, hz + 1)), dma((2, hz + 1)),
-        dma((nz,)), dma((nz,)),
-        dma((ny,)), dma((ny,)),
-        dma((2, nt)), dma((2, nt)),
+        dma((2, hy + 1)), dma((2, hy + 1)),
+        dma((hz + 1,)), dma((hz + 1,)),
+        dma((hz + 1, nt)), dma((hz + 1, nt)),
         dma((nz,)), dma((nz,)),
         dma((nt,)), dma((nt,)),
-        dma((ny,)), dma((ny,)),
+        dma((ny, hz + 1)), dma((ny, hz + 1)),
         dma((replicas,)), dma((replicas,)),
     ]
     hbm = pl.BlockSpec(memory_space=pltpu.HBM)

time: 106 us -> 91 us (0.86)
  Pallas kernels: 104 us -> 89.1 us
    pallas_call x1, Pallas kernels: 104 us -> 89.1 us  [shards(): pl.pallas_call(functools.partial(kernel, (nz, ny, nt)), out_shape=jax.Sha...]
where the time goes in v2:
time: 91 us; the launch traced here: 90.9 us
  Pallas kernels  89.1 us (98%)
  local copies, waits for them, and re-layouts  1.83 us (2%)
    pallas_call x1, Pallas kernels, shards(): pl.pallas_call(functools.partial(kernel, (nz, ny, nt)), out_shape=jax.Sha...  89.1 us
    unnamed x1, local copies, waits for them, and re-layouts  1.83 us

profile of v2, /device:TPU:64, one launch (start us, length us, event | category | flops | bytes accessed | tf_op | source)
XLA Modules:
  0.0 90.9 jit_solution(14882688576932083443)
XLA Ops:
  0.0 89.1 %shard_map.64 = bf16[1024,128]{1,0:T(8,128)(2,1)} custom-call(bf16[256,8192]{1,0:T(8,128)(2,1)} %hid.1, bf16[16384,128]{1,0:T(8,128)(2,1)} %bitcast.6, bf16[4,1024,128]{2,1,0:T(8,128)(2,1)} %down.1, bf16[512,128]{1,0:T(8,128)(2,1)} %bitcast.7, s32[1,256]{1,0:T(1,128)} %bitcast.8, s32[1,256]{1,0:T(1,128)} %bitcast.9), custom_call_target="tpu_custom_call" | custom-call | flops 9663676416 | bytes 9437184 | tf_op jit(solution)/shard_map/pallas_call | solution.py:611
  89.1 1.8 %copy.8 = bf16[512,2,128]{2,1,0:T(2,128)(2,1)} copy(bf16[512,2,128]{2,1,0:T(2,128)(2,1)} %bitcast.5) | data formatting | bytes 524288

commit v3 on v2

--- a/solution.py
+++ b/solution.py
@@ -31,9 +31,9 @@
     dims,
     hid, kvw, down, up, idx, dest,
     out,
-    hf, kvb, kvf, base, hbuf, wbuf, upz, colbuf, idz, idy, acc, halves, part, rs, sh, hm, sr, upsend, upsel, bd, perm, kvs,
+    hf, kvb, kvf, base, hbuf, wbuf, upz, colbuf, idz, idy, acc, halves, part, rs, lasts, sh, hm, sr, uses, upsend, upsel, bd, perm, kvs,
     local_sem, z_send, z_recv, w_send, w_recv, u_send, u_recv, i_send, i_recv, j_send, j_recv,
-    p_send, p_recv, a_send, a_recv, b_send, b_recv, c_send, c_recv, s_send, s_recv, o_send, o_recv,
+    l_send, l_recv, p_send, p_recv, a_send, a_recv, b_send, b_recv, c_send, c_recv, s_send, s_recv, o_send, o_recv,
 ):
     nz, ny, nt = dims
     rows, width = hbuf.shape[1], hbuf.shape[2]
@@ -238,8 +238,9 @@
     own_k.wait()
     lax.fori_loop(0, nt, lambda c, _: (full_copy(c).wait(), 0)[1], 0)
 
+    last = hz
     groups = [(0, 1)] + [(2 * s - 1, 2 * s + 1) for s in range(1, hz)] + [(nz - 1, nz)]
-    state = {"base": 0, "w": 0}
+    state = {"base": 0, "w": 0, "up": 0}
     here_k, here_m = {0}, {0}
     pending = {(k, m) for k in range(nz) for m in range(ny)}
     w_waits = [
@@ -250,6 +251,63 @@
         half = adapters // 2
         w_waits += [[(way, 2, w_order[way][n]) for way in range(2)] for n in range(half)]
     w_waits = [pair for pair in w_waits if pair]
+
+    def mark_uses(e, wanted):
+        count = nz * adapters
+        row = lax.broadcasted_iota(jnp.int32, (count, rows), 0)
+        number = jnp.zeros((count, rows), jnp.int32)
+        for k in range(nz):
+            first = (((z + shift_of(k, nz)) % nz) * ny + y) * adapters
+            here = (row >= k * adapters) & (row < (k + 1) * adapters)
+            number = jnp.where(here, first + row - k * adapters, number)
+        found = jnp.where(number == jnp.broadcast_to(wanted, (count, rows)), 1.0, 0.0)
+        uses[e] = jnp.broadcast_to(jnp.max(found, axis=1, keepdims=True), (count, 128))
+
+    def select_up(e, into, low, high):
+        for k in range(low, high):
+            total = jnp.zeros((rank, 128), F32)
+            for j in range(adapters):
+                at = k * adapters + j
+                total = total + uses[e, at : at + 1] * upz[k, j * rank : (j + 1) * rank].astype(F32)
+            into[k] = total.astype(BF16)
+
+    u_groups = groups
+
+    def s_copy(d, g):
+        span = pl.ds(u_groups[g][0], u_groups[g][1] - u_groups[g][0])
+        return remote(
+            upsend.at[d, span], upsel.at[(-d) % ny, span], s_send.at[d, g], s_recv.at[d, g], at_y(d), t
+        )
+
+    rank_half = (lax.broadcasted_iota(jnp.int32, (rank, 128), 0) < rank // 2).astype(F32)
+
+    def spread_up(e, g):
+        def one(k, _):
+            block = upsel[e, k].astype(F32)
+            at = pl.ds(pl.multiple_of(k * rank, rank), rank)
+            bd[e, at, 0:128] = (block * rank_half).astype(BF16)
+            bd[e, at, 128:256] = (block * (1.0 - rank_half)).astype(BF16)
+            return 0
+
+        lax.fori_loop(u_groups[g][0], u_groups[g][1], one, 0)
+
+    def u_group(g):
+        for d in range(1, ny):
+            select_up(d, upsend.at[d], *u_groups[g])
+            s_copy(d, g).start()
+        select_up(0, upsel.at[0], *u_groups[g])
+        spread_up(0, g)
+
+    def early_up():
+        if state["up"]:
+            return
+        state["up"] = 1
+        j_copy(0, hy).wait_recv()
+        own_u.wait()
+        mark_uses(0, idx[...])
+        for d in range(1, ny):
+            mark_uses(d, idy[d])
+        u_group(0)
 
     def some_units(budget):
         while budget > 0:
@@ -309,6 +367,8 @@
                             j_copy(way, step + 1).start()
             if not some_base(3):
                 some_units(4)
+            if step == hy and c == 2:
+                early_up()
     while state["w"] < len(w_waits):
         next_w()
     some_base(nt)
@@ -332,8 +392,19 @@
         part[low:high] = acc[low:high, core] + halves[low:high]
         lax.fori_loop(1, nx, lambda i, _: (a_copy(i, g).start(), 0)[1], 0)
 
+    def l_copy(i):
+        to = (t + i) % nt
+        return remote(acc.at[nz - 1, to % 2, to // 2], lasts.at[i], l_send.at[i], l_recv.at[i], r, to)
+
     def finish_a(g):
         low, high = groups[g]
+        if g == last:
+            lax.fori_loop(1, nt, lambda i, _: (l_copy(i).wait_recv(), 0)[1], 0)
+            total = acc[nz - 1, core, x]
+            for i in range(1, nt):
+                total = total + lasts[i]
+            sh[nz - 1] = total.astype(BF16)
+            return
         lax.fori_loop(1, nx, lambda i, _: (a_copy(i, g).wait_recv(), 0)[1], 0)
         total = part[low:high, x]
         for i in range(1, nx):
@@ -367,40 +438,10 @@
                 for m in ms:
                     units(k, k + 1, m, m + 1)
                     pending.discard((k, m))
-        p_copy(g).start()
-
-    def select_up(wanted, into, low, high):
-        def one(k, _):
-            first = (((z + shift_of(k, nz)) % nz) * ny + y) * adapters
-            total = jnp.zeros((rank, 128), F32)
-            for j in range(adapters):
-                uses = jnp.where(wanted == first + j, 1.0, 0.0)
-                uses = jnp.max(uses, axis=1, keepdims=True)
-                total = total + uses * upz[k, j * rank : (j + 1) * rank].astype(F32)
-            into[k] = total.astype(BF16)
-            return 0
-
-        lax.fori_loop(low, high, one, 0)
-
-    u_groups = groups
-
-    def s_copy(d, g):
-        span = pl.ds(u_groups[g][0], u_groups[g][1] - u_groups[g][0])
-        return remote(
-            upsend.at[d, span], upsel.at[(-d) % ny, span], s_send.at[d, g], s_recv.at[d, g], at_y(d), t
-        )
-
-    rank_half = (lax.broadcasted_iota(jnp.int32, (rank, 128), 0) < rank // 2).astype(F32)
-
-    def spread_up(e, g):
-        def one(k, _):
-            block = upsel[e, k].astype(F32)
-            at = pl.ds(pl.multiple_of(k * rank, rank), rank)
-            bd[e, at, 0:128] = (block * rank_half).astype(BF16)
-            bd[e, at, 128:256] = (block * (1.0 - rank_half)).astype(BF16)
-            return 0
-
-        lax.fori_loop(u_groups[g][0], u_groups[g][1], one, 0)
+        if g < last:
+            p_copy(g).start()
+        else:
+            lax.fori_loop(1, nt, lambda i, _: (l_copy(i).start(), 0)[1], 0)
 
     def u_pass(step):
         for h in range(2):
@@ -410,13 +451,6 @@
                     if u_takes(way, step + 1, h):
                         u_copy(way, step + 1, h).start()
 
-    def u_group(g):
-        for d in range(1, ny):
-            select_up(idy[d], upsend.at[d], *u_groups[g])
-            s_copy(d, g).start()
-        select_up(idx[...], upsel.at[0], *u_groups[g])
-        spread_up(0, g)
-
     def s_finish(g):
         for d in range(1, ny):
             s_copy(d, g).wait_recv()
@@ -427,10 +461,7 @@
             j_copy(way, step).wait_recv()
             if once(way, step + 1, hy):
                 j_copy(way, step + 1).start()
-    j_copy(0, hy).wait_recv()
-    own_u.wait()
-    u_group(0)
-    last = len(groups) - 1
+    early_up()
     for g in range(last):
         rest_of(g)
         if g:
@@ -441,21 +472,20 @@
         if c == 0:
             u_pass(1)
             pass_on(last - 1)
-            u_group(1)
     i_copy(0, hz).wait_recv()
     wide_column(nz - 1, idz[nz - 1])
     rest_of(last)
     for g in range(last):
         finish(g)
-    pass_on(last)
+    u_group(1)
     if hz > 1:
         u_pass(2)
     finish(last)
-    for step in range(2, hz):
+    if hz > 1:
+        u_group(2)
+    for step in range(3, hz):
+        u_pass(step)
         u_group(step)
-        u_pass(step + 1)
-    if hz > 1:
-        u_group(hz)
 
     for k in range(1, nz):
         b_copy(k).wait_recv()
@@ -473,6 +503,9 @@
         return remote(sr.at[at], sr.at[at], c_send.at[i], c_recv.at[i], r, src)
 
     lax.fori_loop(1, nt, lambda i, _: (c_copy(i).start(), 0)[1], 0)
+    if hz > 2:
+        u_pass(hz)
+        u_group(hz)
     for g in range(hz + 1):
         s_finish(g)
     lax.fori_loop(1, nt, lambda i, _: (c_arrival(i).wait_recv(), 0)[1], 0)
@@ -498,20 +531,20 @@
     kvs[...] = cache.reshape(replicas, cap2, 128)
 
     def o_copy(i):
-        to = (r + i) % replicas
+        to = ((z + shift_of(i // ny, nz)) % nz) * ny + (y + i % ny) % ny
         return remote(
             kvs.at[to], out.at[pl.ds(pl.multiple_of(r * cap2, cap2), cap2)],
             o_send.at[i], o_recv.at[i], to, t,
         )
 
     def o_arrival(i):
-        src = (r + replicas - i) % replicas
+        src = ((z + nz - shift_of(i // ny, nz)) % nz) * ny + (y + ny - i % ny) % ny
         return remote(
             kvs.at[src], out.at[pl.ds(pl.multiple_of(src * cap2, cap2), cap2)],
             o_send.at[i], o_recv.at[i], src, t,
         )
 
-    lax.fori_loop(1, replicas, lambda i, _: (o_copy(i).start(), 0)[1], 0)
+    lax.fori_loop(1, replicas, lambda i, _: (o_copy(replicas - i).start(), 0)[1], 0)
     own_o = pltpu.make_async_copy(
         kvs.at[r], out.at[pl.ds(pl.multiple_of(r * cap2, cap2), cap2)], local_sem.at[4 + nt]
     )
@@ -541,10 +574,11 @@
 
     def tensor_sends(i, _):
         c_copy(i).wait_send()
+        l_copy(i).wait_send()
         return 0
 
     lax.fori_loop(1, nt, tensor_sends, 0)
-    for g in range(len(groups)):
+    for g in range(last):
         p_copy(g).wait_send()
         lax.fori_loop(1, nx, lambda i, _, g=g: (a_copy(i, g).wait_send(), 0)[1], 0)
 
@@ -585,9 +619,11 @@
         vm((nz, nt // 2, sub, rank), F32),
         vm((nz, nt // 2, sub, rank), F32),
         vm((nt // 2, nz, sub, rank), F32),
+        vm((nt, sub, rank), F32),
         vm((nz, sub, rank), BF16),
         vm((nz, sub, rank), BF16),
         vm((nt, sub, rank), BF16),
+        vm((ny, nz * adapters, 128), F32),
         vm((ny, nz, rank, cols), BF16),
         vm((ny, nz, rank, cols), BF16),
         vm((ny, nz * rank, 2 * cols), BF16),
@@ -599,6 +635,7 @@
         dma((2, hz + 1, 2)), dma((2, hz + 1, 2)),
         dma((2, hz + 1)), dma((2, hz + 1)),
         dma((2, hy + 1)), dma((2, hy + 1)),
+        dma((nt,)), dma((nt,)),
         dma((hz + 1,)), dma((hz + 1,)),
         dma((hz + 1, nt)), dma((hz + 1, nt)),
         dma((nz,)), dma((nz,)),
@@ -610,9 +647,9 @@
     in_vmem = pl.BlockSpec(memory_space=pltpu.VMEM)
     cache = pl.pallas_call(
         functools.partial(kernel, (nz, ny, nt)),
-        out_shape=jax.ShapeDtypeStruct((replicas * cap2, cols), BF16),
+        out_shape=pltpu.VMEM((replicas * cap2, cols), BF16),
         in_specs=[hbm, hbm, hbm, hbm, in_vmem, in_vmem],
-        out_specs=hbm,
+        out_specs=in_vmem,
         scratch_shapes=scratch,
         compiler_params=pltpu.CompilerParams(
             collective_id=0, has_side_effects=True, vmem_limit_bytes=56 * 1024 * 1024

time: 91 us -> 87.8 us (0.965)
  Pallas kernels: 89.1 us -> 86.1 us
  local copies, waits for them, and re-layouts: 1.83 us -> 0.71 us
    pallas_call x1, Pallas kernels: 89.1 us -> 86.1 us  [shards(): pl.pallas_call(functools.partial(kernel, (nz, ny, nt)), out_shape=pltpu.V...]
    unnamed x1, local copies, waits for them, and re-layouts: 1.83 us -> 0.71 us
where the time goes in v3:
time: 87.8 us; the launch traced here: 86.8 us
  Pallas kernels  86.1 us (98%)
    pallas_call x1, Pallas kernels, shards(): pl.pallas_call(functools.partial(kernel, (nz, ny, nt)), out_shape=pltpu.V...  86.1 us

profile of v3, /device:TPU:64, one launch (start us, length us, event | category | flops | bytes accessed | tf_op | source)
XLA Modules:
  0.0 86.8 jit_solution(10460552840767678333)
XLA Ops:
  0.0 86.1 %shard_map.64 = bf16[1024,128]{1,0:T(8,128)(2,1)S(1)} custom-call(bf16[256,8192]{1,0:T(8,128)(2,1)} %hid.1, bf16[16384,128]{1,0:T(8,128)(2,1)} %bitcast.6, bf16[4,1024,128]{2,1,0:T(8,128)(2,1)} %down.1, bf16[512,128]{1,0:T(8,128)(2,1)} %bitcast.7, s32[1,256]{1,0:T(1,128)} %bitcast.8, s32[1,256]{1,0:T(1,128)} %bitcast.9), custom_call_target="tpu_custom_call" | custom-call | flops 9663676416 | bytes 9437184 | tf_op jit(solution)/shard_map/pallas_call | solution.py:648
  86.1 0.7 copy.8

commit v4 on v3

--- a/solution.py
+++ b/solution.py
@@ -63,6 +63,16 @@
             device_id=(replica, tensor), device_id_type=MESH,
         )
 
+    barrier = pltpu.get_barrier_semaphore()
+
+    def greet_tensor(i, _):
+        pl.semaphore_signal(barrier, inc=1, device_id=(r, (t + i) % nt), device_id_type=MESH)
+        return 0
+
+    for to in (at_z(1), at_z(-1), at_y(1), at_y(-1)):
+        pl.semaphore_signal(barrier, inc=1, device_id=(to, t), device_id_type=MESH)
+    lax.fori_loop(1, nt, greet_tensor, 0)
+
     own_cols = pl.ds(pl.multiple_of(t * width, 128), width)
     own_h = pltpu.make_async_copy(hid.at[:, own_cols], hbuf.at[0], local_sem.at[0])
     own_w = pltpu.make_async_copy(down, wbuf.at[0], local_sem.at[1])
@@ -80,15 +90,6 @@
     own_k.start()
     lax.fori_loop(0, nt, lambda c, _: (full_copy(c).start(), 0)[1], 0)
 
-    barrier = pltpu.get_barrier_semaphore()
-
-    def greet_tensor(i, _):
-        pl.semaphore_signal(barrier, inc=1, device_id=(r, (t + i) % nt), device_id_type=MESH)
-        return 0
-
-    for to in (at_z(1), at_z(-1), at_y(1), at_y(-1)):
-        pl.semaphore_signal(barrier, inc=1, device_id=(to, t), device_id_type=MESH)
-    lax.fori_loop(1, nt, greet_tensor, 0)
     pl.semaphore_wait(barrier, 4 + nt - 1)
 
     def z_copy(way, step, c):
@@ -513,19 +514,16 @@
     shrink = sr[...].astype(F32).reshape(rows, rank)
     wanted = colbuf[0]
 
-    def delta_part(e, _):
+    total = base[...]
+    for e in range(ny):
         parts = []
         for k in range(nz):
-            d = shift_of(k, nz)
-            first = (((z + d) % nz) * ny + (y + e) % ny) * adapters
-            uses = (wanted >= first) & (wanted < first + adapters)
-            parts.append(jnp.where(uses, shrink, 0.0).astype(BF16))
+            first = (((z + shift_of(k, nz)) % nz) * ny + (y + e) % ny) * adapters
+            uses_it = (wanted >= first) & (wanted < first + adapters)
+            parts.append(jnp.where(uses_it, shrink, 0.0).astype(BF16))
         spread = jnp.concatenate(parts, axis=1)
-        base[...] += SCALE * jnp.dot(spread, bd[e], preferred_element_type=F32)
-        return 0
-
-    lax.fori_loop(0, ny, delta_part, 0)
-    projected = base[...].astype(BF16)
+        total = total + SCALE * jnp.dot(spread, bd[e], preferred_element_type=F32)
+    projected = total.astype(BF16)
     stacked = jnp.concatenate([projected[:, 0:128], projected[:, 128:256]], axis=0)
     cache = jnp.dot(perm[...], stacked, preferred_element_type=F32).astype(BF16)
     kvs[...] = cache.reshape(replicas, cap2, 128)

time: 87.8 us -> 87.1 us (level)
  no operation moved by 1% of the time
where the time goes in v4:
time: 87.1 us; the launch traced here: 86 us
  Pallas kernels  85.3 us (98%)
    pallas_call x1, Pallas kernels, shards(): pl.pallas_call(functools.partial(kernel, (nz, ny, nt)), out_shape=pltpu.V...  85.3 us

profile of v4, /device:TPU:64, one launch (start us, length us, event | category | flops | bytes accessed | tf_op | source)
XLA Modules:
  0.0 86.0 jit_solution(8102841360688493188)
XLA Ops:
  0.0 85.3 %shard_map.64 = bf16[1024,128]{1,0:T(8,128)(2,1)S(1)} custom-call(bf16[256,8192]{1,0:T(8,128)(2,1)} %hid.1, bf16[16384,128]{1,0:T(8,128)(2,1)} %bitcast.6, bf16[4,1024,128]{2,1,0:T(8,128)(2,1)} %down.1, bf16[512,128]{1,0:T(8,128)(2,1)} %bitcast.7, s32[1,256]{1,0:T(1,128)} %bitcast.8, s32[1,256]{1,0:T(1,128)} %bitcast.9), custom_call_target="tpu_custom_call" | custom-call | flops 9663676416 | bytes 9437184 | tf_op jit(solution)/shard_map/pallas_call | solution.py:646
  85.3 0.7 copy.8

commit v5 on v4

--- a/solution.py
+++ b/solution.py
@@ -487,6 +487,8 @@
     for step in range(3, hz):
         u_pass(step)
         u_group(step)
+        s_finish(step - 3)
+        s_finish(step - 2)
 
     for k in range(1, nz):
         b_copy(k).wait_recv()
@@ -507,7 +509,7 @@
     if hz > 2:
         u_pass(hz)
         u_group(hz)
-    for g in range(hz + 1):
+    for g in range(2 if hz > 3 else 0, hz + 1):
         s_finish(g)
     lax.fori_loop(1, nt, lambda i, _: (c_arrival(i).wait_recv(), 0)[1], 0)
 

time: 87.1 us -> 87.1 us (level)
  no operation moved by 1% of the time
where the time goes in v5:
time: 87.1 us; the launch traced here: 86 us
  Pallas kernels  85.3 us (98%)
    pallas_call x1, Pallas kernels, shards(): pl.pallas_call(functools.partial(kernel, (nz, ny, nt)), out_shape=pltpu.V...  85.3 us

profile of v5, /device:TPU:64, one launch (start us, length us, event | category | flops | bytes accessed | tf_op | source)
XLA Modules:
  0.0 86.0 jit_solution(12535677345673798937)
XLA Ops:
  0.0 85.3 %shard_map.64 = bf16[1024,128]{1,0:T(8,128)(2,1)S(1)} custom-call(bf16[256,8192]{1,0:T(8,128)(2,1)} %hid.1, bf16[16384,128]{1,0:T(8,128)(2,1)} %bitcast.6, bf16[4,1024,128]{2,1,0:T(8,128)(2,1)} %down.1, bf16[512,128]{1,0:T(8,128)(2,1)} %bitcast.7, s32[1,256]{1,0:T(1,128)} %bitcast.8, s32[1,256]{1,0:T(1,128)} %bitcast.9), custom_call_target="tpu_custom_call" | custom-call | flops 9663676416 | bytes 9437184 | tf_op jit(solution)/shard_map/pallas_call | solution.py:648
  85.3 0.7 copy.8
